TPU v7x, 128 devices: a whole 4x4x4 slice. The times are simulated.
128 devices in a mesh: space: 16 (over x, z_lo, core), instance: 4 (over y), coarse: 2 (over z_hi).
Axes of the slice: x: 4, y: 4, z: 4 (z_hi: 2, z_lo: 2; z = z_hi * 2 + z_lo), core: 2. Of those that a mesh axis runs over, the one named last changes fastest.
Arguments:
- forcing: float32 [8, 5, 128, 32, 512], P('instance', None, 'space', 'coarse'), may hold values from -6 to 6
- state_start: float32 [8, 5, 128, 32, 512], P('instance', None, 'space', 'coarse'), may hold values from -6 to 6
- kappa: float32 [128, 32, 512], P('space', 'coarse'), may hold values from 0.25 to 4
- coupling: float32 [5, 5], replicated, may hold values from -1.25 to 1.25
- lag: int32 [32], P('coarse'), may hold values from 0 to 7
Outputs:
- state: float32 [8, 5, 128, 32, 512], P('instance', None, 'space', 'coarse')
All inputs are finite; a program needn't handle non-finite values.
Results may differ from a plain program's by a relative error of at most 0.0001.
Values sent between devices are 32-bit elements; how exact they have to be, the bound alone decides.
A program may use at most 192 MiB of HBM per device.

v0:
```python
import jax
import jax.numpy as jnp
from jax import lax
from jax.sharding import PartitionSpec as P

FINE_CYCLES = 2
COARSE_SWEEPS = 2


HIGH = lax.Precision.HIGHEST


def with_halo(value, sides, width):
    for axis, dim in sides:
        count, length = (lax.axis_size(axis), value.shape[dim])
        up = [(i, (i + 1) % count) for i in range(count - 1)]
        down = [(j, i) for i, j in up]
        last = lax.slice_in_dim(value, length - width, length, axis=dim)
        leading = lax.slice_in_dim(value, 0, width, axis=dim)
        before = lax.ppermute(last, axis, up)
        after = lax.ppermute(leading, axis, down)
        value = jnp.concatenate([before, value, after], axis=dim)
    return value


def spectral_matrix(count):
    diff = jnp.arange(count, dtype=jnp.int32)[:, None] - jnp.arange(count, dtype=jnp.int32)[None, :]
    sign = (1 - 2 * (jnp.abs(diff) % 2)).astype(jnp.float32)
    angle = jnp.pi * diff.astype(jnp.float32) / count
    sine = jnp.where(diff == 0, jnp.float32(1.0), jnp.sin(angle))
    return jnp.where(diff == 0, jnp.float32(0.0), 0.5 * sign * jnp.cos(angle) / sine)


def residual_of(field, source, low_ghost, high_ghost, forcing, kappa, coupling):
    padded = with_halo(field, (("space", 2), ("coarse", 3)), 1)
    beside = padded[:, :, 2:, 1:-1] + padded[:, :, :-2, 1:-1]
    beside = beside + padded[:, :, 1:-1, 2:] + padded[:, :, 1:-1, :-2]
    length = field.shape[4]
    column = jnp.arange(length, dtype=jnp.int32)
    upper = jnp.where(column == length - 1, high_ghost[..., None], jnp.roll(field, -1, axis=4))
    lower = jnp.where(column == 0, low_ghost[..., None], jnp.roll(field, 1, axis=4))
    mixed = jnp.einsum("cd,ndxzy->ncxzy", coupling, field, precision=HIGH)
    return forcing - source - (6.0 + kappa) * field + beside + upper + lower - mixed


def coarse_apply(field, padded, kappa_c, coupling):
    beside = padded[:, :, 2:, 1:-1] + padded[:, :, :-2, 1:-1]
    beside = beside + padded[:, :, 1:-1, 2:] + padded[:, :, 1:-1, :-2]
    beside = beside + jnp.roll(field, 1, axis=4) + jnp.roll(field, -1, axis=4)
    mixed = jnp.einsum("cd,ndxzy->ncxzy", coupling, field, precision=HIGH)
    return (6.0 + kappa_c) * field - beside + mixed


def shards(forcing, state_start, kappa, coupling, lag):
    inst_dev, comps, cells_x, cells_z, cells_y = state_start.shape
    count = inst_dev * lax.axis_size("instance")
    first_own = lax.axis_index("instance") * inst_dev
    owned = first_own + jnp.arange(inst_dev, dtype=jnp.int32)
    rows = lax.dynamic_slice_in_dim(spectral_matrix(count), first_own, inst_dev, 0)
    low_idx = (owned[:, None] - lag[None, :]) % count
    high_idx = (owned[:, None] + lag[None, :]) % count
    piece = lax.all_gather(state_start, "instance", axis=0, tiled=True)
    width = piece.shape[0]
    columns = jnp.arange(width, dtype=jnp.int32)
    source = jnp.einsum("nk,kcxzy->ncxzy", rows, piece, precision=HIGH)
    low_pick = (low_idx[:, None, :] == columns[None, :, None]).astype(jnp.float32)
    high_pick = (high_idx[:, None, :] == columns[None, :, None]).astype(jnp.float32)
    low_ghost = jnp.einsum("nkz,kcxz->ncxz", low_pick, piece[:, :, :, :, -1], precision=HIGH)
    high_ghost = jnp.einsum("nkz,kcxz->ncxz", high_pick, piece[:, :, :, :, 0], precision=HIGH)
    source, low_ghost, high_ghost = (source, low_ghost, high_ghost)
    step = 0.8 / (6.0 + kappa)
    field = state_start
    for cycle in range(FINE_CYCLES):
        begin = field
        for weight in (0.25, 0.5, 1.0):
            field = begin + weight * step * residual_of(
                field, source, low_ghost, high_ghost, forcing, kappa, coupling
            )
    last = residual_of(field, source, low_ghost, high_ghost, forcing, kappa, coupling)
    half_x, half_z, half_y = (cells_x // 2, cells_z // 2, cells_y // 2)
    rhs_c = last.reshape(inst_dev, comps, half_x, 2, half_z, 2, half_y, 2).sum(axis=(3, 5, 7))
    kappa_c = kappa.reshape(half_x, 2, half_z, 2, half_y, 2).mean(axis=(1, 3, 5))
    corr = jnp.zeros_like(rhs_c)
    for sweep in range(COARSE_SWEEPS):
        padded = with_halo(corr, (("space", 2), ("coarse", 3)), 1)
        corr = corr + 0.8 / (6.0 + kappa_c) * (
            rhs_c - coarse_apply(corr, padded, kappa_c, coupling)
        )
    fine_corr = jnp.broadcast_to(
        corr[:, :, :, None, :, None, :, None], (inst_dev, comps, half_x, 2, half_z, 2, half_y, 2)
    )
    return field + fine_corr.reshape(inst_dev, comps, cells_x, cells_z, cells_y)


def solution(mesh):
    return jax.shard_map(
        shards,
        mesh=mesh,
        in_specs=(
            P("instance", None, "space", "coarse", None),
            P("instance", None, "space", "coarse", None),
            P("space", "coarse", None),
            P(),
            P("coarse"),
        ),
        out_specs=P("instance", None, "space", "coarse", None),
        check_vma=False,
    )
```

profile of v0, /device:TPU:100, one launch (start us, length us, event | category | flops | bytes accessed | tf_op | source)
XLA Modules:
  0.0 624.8 jit_solution(2956656567772812338)
XLA Ops:
  17.6 3.9 collective-permute-start.1
  23.6 18.1 %reshape.94 = f32[4,2,8,2,256,2]{5,4,3,2,1,0:T(8,128)} reshape(f32[8,16,512]{2,1,0:T(8,128)S(1)} %copy-done.6) | data formatting | bytes 524288 | tf_op jit(solution)/shard_map/reshape | solution.py:82
  41.7 7.2 %reduce_sum.18 = f32[4,8,256]{2,1,0:T(8,128)S(1)} reduce(f32[4,2,8,2,256,2]{5,4,3,2,1,0:T(8,128)} %reshape.94, f32[]{:T(128)} %constant.62.clone.1), dimensions={1,3,5}, to_apply=%region_0.1 | reduce | flops 57344 | bytes 294916 | tf_op jit(solution)/shard_map/reduce_sum | solution.py:82
  54.8 9.2 %fusion.143 = (f32[2,5,8,16,511]{4,0,3,2,1:T(2,128)}, f32[2,5,8,16,511]{4,0,3,2,1:T(2,128)}) fusion(f32[2,5,8,16,512]{4,0,3,2,1:T(2,128)} %copy.106), kind=kLoop, calls=%fused_computation.283 | loop fusion | bytes 10465280 | tf_op jit(solution)/shard_map/jit(_roll_static)/slice | solution.py:40
  64.0 6.7 %fusion.14 = f32[2,8,16,512,5]{3,4,2,1,0:T(8,128)} fusion(f32[2,5,8,16,512]{4,3,2,1,0:T(8,128)S(1)} %copy-done.1, f32[5,5]{1,0:T(8,128)S(1)} %copy-done), kind=kOutput, calls=%fused_computation.14 | convolution fusion | flops 39321600 | bytes 5242980 | tf_op jit(solution)/shard_map/cd,ndxzy->ncxzy/dot_general | solution.py:42
  85.1 7.4 %collective-permute-start.2 = (f32[2,5,10,1,512]{4,0,3,2,1:T(2,128)}, f32[2,5,10,1,512]{4,0,3,2,1:T(2,128)}, u32[]{:S(2)}, u32[]{:S(2)}) collective-permute-start(f32[2,5,10,1,512]{4,0,3,2,1:T(2,128)} %get-tuple-element.19), channel_id=1, source_target_pairs={{1,0},{3,2},{5,4},{7,6},{9,8},{11,10},{13,12},{15,14},{17,16},{19,... | collective-permute-start | bytes 614408 | tf_op jit(solution)/shard_map/ppermute | solution.py:21
  93.8 17.4 %all-gather.2.cloned.1.call-done = f32[8,5,8,16,512]{4,3,2,1,0:T(8,128)} async-done(((f32[2,5,8,16,512]{4,3,2,1,0:T(8,128)}), f32[8,5,8,16,512]{4,3,2,1,0:T(8,128)}) %all-gather.2.cloned.1.call-update) | async-done | bytes 10485776 | tf_op jit(solution)/shard_map/all_gather | solution.py:62
  111.2 5.8 fusion.122
  116.9 5.5 copy.127
  123.4 5.5 copy.128
  131.3 37.0 %multiply_add_fusion.5 = (f32[2,5,8,16,512]{4,0,3,2,1:T(2,128)S(1)}, f32[2,5,8,16,512]{4,0,3,2,1:T(2,128)S(1)}) fusion(f32[2,5,8,16,512]{4,0,3,2,1:T(2,128)} %copy.106, f32[2,8,16,512,5]{3,4,2,1,0:T(8,128)} %fusion.14, f32[2,5,8,16,511]{4,0,3,2,1:T(2,128)} %get-tuple-element.60, f32[2,5,8,16,1]{4,0,3,2,1:T(2,128)} %get-tuple-element.62, ...), kind=kOutput, calls=%fused_computation.137 | convolution fusion | flops 76021760 | bytes 36597764 | tf_op jit(solution)/shard_map/nk,kcxzy->ncxzy/dot_general | solution.py:65
  168.6 5.5 fusion.12
  178.5 4.2 fusion.140
  182.7 4.3 collective-permute-done.5
  193.6 5.9 collective-permute-done.7
  199.5 14.6 %multiply_add_fusion.4 = f32[2,5,8,16,512]{4,0,3,2,1:T(2,128)S(1)} fusion(f32[2,8,16,512,5]{3,4,2,1,0:T(8,128)S(1)} %fusion.12, f32[2,5,8,16,511]{4,0,3,2,1:T(2,128)S(1)} %get-tuple-element.54, f32[2,5,8,16,1]{4,0,3,2,1:T(2,128)S(1)} %get-tuple-element.56, pred[512]{0:T(512)(128)(4,1)S(1)} %get-tuple-element.84, ...), kind=kLoop, calls=%fused_computation.136 | loop fusion | flops 15073280 | bytes 19950592 | tf_op jit(solution)/shard_map/add | solution.py:76
  214.4 5.5 fusion.10
  224.2 4.2 fusion.137
  236.0 5.9 collective-permute-done.11
  241.9 14.4 %multiply_add_fusion.3 = f32[2,5,8,16,512]{4,0,3,2,1:T(2,128)S(1)} fusion(f32[2,8,16,512,5]{3,4,2,1,0:T(8,128)S(1)} %fusion.10, f32[2,5,8,16,511]{4,0,3,2,1:T(2,128)S(1)} %get-tuple-element.48, f32[2,5,8,16,1]{4,0,3,2,1:T(2,128)S(1)} %get-tuple-element.50, pred[512]{0:T(512)(128)(4,1)S(1)} %get-tuple-element.84, ...), kind=kLoop, calls=%fused_computation.135 | loop fusion | flops 15073280 | bytes 19950592 | tf_op jit(solution)/shard_map/add | solution.py:76
  256.6 5.5 fusion.8
  267.8 3.9 fusion.134
  279.6 5.9 collective-permute-done.15
  285.5 13.2 %multiply_add_fusion.2 = f32[2,5,8,16,512]{4,0,3,2,1:T(2,128)S(1)} fusion(f32[2,5,8,16,512]{4,0,3,2,1:T(2,128)S(1)} %multiply_add_fusion.3, f32[2,8,16,512,5]{3,4,2,1,0:T(8,128)S(1)} %fusion.8, f32[2,5,8,16,511]{4,0,3,2,1:T(2,128)S(1)} %get-tuple-element.42, f32[2,5,8,16,1]{4,0,3,2,1:T(2,128)S(1)} %get-tuple-element.44, ...), kind=kLoop, calls=%fused_computation.134 | loop fusion | flops 15073280 | bytes 17329152 | tf_op jit(solution)/shard_map/add | solution.py:76
  299.0 5.5 fusion.6
  304.5 4.6 collective-permute-start.16
  311.5 4.2 fusion.131
  323.1 5.9 collective-permute-done.19
  329.1 14.3 %multiply_add_fusion.1 = f32[2,5,8,16,512]{4,0,3,2,1:T(2,128)S(1)} fusion(f32[2,5,8,16,512]{4,0,3,2,1:T(2,128)S(1)} %multiply_add_fusion.3, f32[2,8,16,512,5]{3,4,2,1,0:T(8,128)S(1)} %fusion.6, f32[2,5,8,16,511]{4,0,3,2,1:T(2,128)S(1)} %get-tuple-element.36, f32[2,5,8,16,1]{4,0,3,2,1:T(2,128)S(1)} %get-tuple-element.38, ...), kind=kLoop, calls=%fused_computation.133 | loop fusion | flops 15073280 | bytes 19950592 | tf_op jit(solution)/shard_map/add | solution.py:76
  343.6 5.5 fusion.4
  349.1 4.1 collective-permute-start.20
  355.4 4.2 fusion.128
  367.5 5.9 collective-permute-done.23
  373.4 14.1 %multiply_add_fusion = f32[2,5,8,16,512]{4,0,3,2,1:T(2,128)S(1)} fusion(f32[2,5,8,16,512]{4,0,3,2,1:T(2,128)S(1)} %multiply_add_fusion.3, f32[2,8,16,512,5]{3,4,2,1,0:T(8,128)S(1)} %fusion.4, f32[2,5,8,16,511]{4,0,3,2,1:T(2,128)S(1)} %get-tuple-element.30, f32[2,5,8,16,1]{4,0,3,2,1:T(2,128)S(1)} %get-tuple-element.32, ...), kind=kLoop, calls=%fused_computation.132 | loop fusion | flops 15073280 | bytes 19950592 | tf_op jit(solution)/shard_map/add | solution.py:76
  387.5 5.5 fusion.2
  393.3 3.9 collective-permute-start.24
  399.3 3.7 fusion.125
  411.4 5.9 collective-permute-done.27
  417.3 14.1 %fusion.20 = f32[2,5,8,16,512]{4,0,3,2,1:T(2,128)} fusion(f32[2,5,10,1,512]{4,0,3,2,1:T(2,128)S(1)} %collective-permute-done.27, f32[2,5,1,16,512]{4,0,3,2,1:T(2,128)S(1)} %collective-permute-done.24, f32[2,5,8,16,512]{4,0,3,2,1:T(2,128)S(1)} %multiply_add_fusion, f32[2,5,1,16,512]{4,0,3,2,1:T(2,128)S(1)} %collective-permute-done.25, ...), kind=kLoop, calls=%fused_computation.21 | loop fusion | flops 13762560 | bytes 17067008 | tf_op jit(solution)/shard_map/sub | solution.py:43
  431.5 34.1 %copy.115 = f32[2,5,8,16,512]{1,4,3,2,0:T(8,128)} copy(f32[2,5,8,16,512]{4,0,3,2,1:T(2,128)} %fusion.20) | data formatting | bytes 5242880 | tf_op jit(solution)/shard_map/sub | solution.py:43
  465.5 47.0 %reduce_sum.19 = f32[2,5,4,8,256]{1,4,3,2,0:T(8,128)} reduce(f32[2,5,4,2,8,2,256,2]{1,7,6,5,4,3,2,0:T(2,128)} %bitcast.20, f32[]{:T(128)} %constant.62.clone.1), dimensions={3,5,7}, to_apply=%region_1.2 | reduce | flops 573440 | bytes 2949124 | tf_op jit(solution)/shard_map/reduce_sum | solution.py:81
  512.5 6.0 copy.116
  520.4 4.1 collective-permute-start.32
  526.9 3.8 collective-permute-done.33
  535.3 5.8 collective-permute-done.35
  542.1 4.8 copy.118
  546.9 26.0 %broadcast_in_dim.159 = f32[2,5,4,2,8,2,256,2]{1,7,6,5,4,3,2,0:T(2,128)} broadcast(f32[2,5,4,8,256]{1,4,3,2,0:T(8,128)} %copy.118), dimensions={0,1,2,4,6} | broadcast | bytes 2949120 | tf_op jit(solution)/shard_map/broadcast_in_dim | solution.py:89
  572.9 39.5 %copy.119 = f32[2,5,8,16,512]{4,0,3,2,1:T(2,128)} copy(f32[2,5,8,16,512]{1,4,3,2,0:T(8,128)} %bitcast.23) | data formatting | bytes 5242880 | tf_op jit(solution)/shard_map/reshape | solution.py:92
  (145 shorter events, 121.0 us)
Async XLA Ops:
  6.5 57.5 %copy-start = (f32[5,5]{1,0:T(8,128)S(1)}, f32[5,5]{1,0:T(8,128)}, u32[]{:S(2)}) copy-start(f32[5,5]{1,0:T(8,128)} %param.8) | copy-start | bytes 304
  6.5 104.6 %all-gather.2.cloned.1.call-start = ((), (), s32[]{:S(2)}) async-start(), calls=%async_computation | async-start | bytes 13107200 | tf_op jit(solution)/shard_map/all_gather | solution.py:62
  7.3 16.3 %copy-start.6 = (f32[8,16,512]{2,1,0:T(8,128)S(1)}, f32[8,16,512]{2,1,0:T(8,128)}, u32[]{:S(2)}) copy-start(f32[8,16,512]{2,1,0:T(8,128)} %param.7) | copy-start | bytes 786436
  7.3 64.7 %collective-permute-start.28 = (f32[2,5,1,8,256]{4,1,3,2,0:T(8,128)S(1)}, f32[2,5,1,8,256]{4,1,3,2,0:T(8,128)S(1)}, u32[]{:S(2)}, u32[]{:S(2)}) collective-permute-start(f32[2,5,1,8,256]{4,1,3,2,0:T(8,128)S(1)} %broadcast.165), channel_id=1, source_target_pairs={{8,0},{16,8},{24,16},{32,24},{40,32},{48,40},{56,48},{64,56},{72,6... | collective-permute-start | bytes 245768 | tf_op jit(solution)/shard_map/ppermute | solution.py:21
  9.4 62.6 %collective-permute-start.29 = (f32[2,5,1,8,256]{4,1,3,2,0:T(8,128)S(1)}, f32[2,5,1,8,256]{4,1,3,2,0:T(8,128)}, u32[]{:S(2)}, u32[]{:S(2)}) collective-permute-start(f32[2,5,1,8,256]{4,1,3,2,0:T(8,128)S(1)} %broadcast.165), channel_id=1, source_target_pairs={{0,8},{8,16},{16,24},{24,32},{32,40},{40,48},{48,56},{56,64},{64,7... | collective-permute-start | bytes 245768 | tf_op jit(solution)/shard_map/ppermute | solution.py:20
  17.6 60.5 %collective-permute-start.1 = (f32[2,5,1,16,512]{4,0,3,2,1:T(2,128)}, f32[2,5,1,16,512]{4,0,3,2,1:T(2,128)}, u32[]{:S(2)}, u32[]{:S(2)}) collective-permute-start(f32[2,5,1,16,512]{4,0,3,2,1:T(2,128)} %get-tuple-element.58), channel_id=1, source_target_pairs={{0,8},{8,16},{16,24},{24,32},{32,40},{40,48},{48,56},{56,64},{64,7... | collective-permute-start | bytes 983048 | tf_op jit(solution)/shard_map/ppermute | solution.py:20
  21.5 60.1 %collective-permute-start = (f32[2,5,1,16,512]{4,0,3,2,1:T(2,128)}, f32[2,5,1,16,512]{4,0,3,2,1:T(2,128)}, u32[]{:S(2)}, u32[]{:S(2)}) collective-permute-start(f32[2,5,1,16,512]{4,0,3,2,1:T(2,128)} %get-tuple-element.57), channel_id=1, source_target_pairs={{8,0},{16,8},{24,16},{32,24},{40,32},{48,40},{56,48},{64,56},{72,6... | collective-permute-start | bytes 983048 | tf_op jit(solution)/shard_map/ppermute | solution.py:21
  41.7 7.7 %copy-start.18 = (s32[16]{0:T(128)S(1)}, s32[16]{0:T(128)}, u32[]{:S(2)}) copy-start(s32[16]{0:T(128)} %param.9) | copy-start | bytes 196
  72.0 9.6 %copy-start.10 = (f32[2,5,1,8,256]{4,1,3,2,0:T(8,128)}, f32[2,5,1,8,256]{4,1,3,2,0:T(8,128)S(1)}, u32[]{:S(2)}) copy-start(f32[2,5,1,8,256]{4,1,3,2,0:T(8,128)S(1)} %collective-permute-done.28) | copy-start | bytes 245764
  72.0 9.5 %copy-start.4 = (f32[2,5,4,8,256]{4,1,3,2,0:T(8,128)}, f32[2,5,4,8,256]{4,1,3,2,0:T(8,128)S(1)}, u32[]{:S(2)}) copy-start(f32[2,5,4,8,256]{4,1,3,2,0:T(8,128)S(1)} %broadcast_in_dim.158) | copy-start | bytes 983044
  73.5 445.0 %collective-permute-start.30 = (f32[2,5,6,1,256]{4,1,3,2,0:T(8,128)}, f32[2,5,6,1,256]{4,1,3,2,0:T(8,128)}, u32[]{:S(2)}, u32[]{:S(2)}) collective-permute-start(f32[2,5,6,1,256]{4,1,3,2,0:T(8,128)} %get-tuple-element.65), channel_id=1, source_target_pairs={{1,0},{3,2},{5,4},{7,6},{9,8},{11,10},{13,12},{15,14},{17,16},{19,... | collective-permute-start | bytes 184328 | tf_op jit(solution)/shard_map/ppermute | solution.py:21
  76.6 441.9 %collective-permute-start.31 = (f32[2,5,6,1,256]{4,1,3,2,0:T(8,128)}, f32[2,5,6,1,256]{4,1,3,2,0:T(8,128)}, u32[]{:S(2)}, u32[]{:S(2)}) collective-permute-start(f32[2,5,6,1,256]{4,1,3,2,0:T(8,128)} %get-tuple-element.66), channel_id=1, source_target_pairs={{0,1},{2,3},{4,5},{6,7},{8,9},{10,11},{12,13},{14,15},{16,17},{18,... | collective-permute-start | bytes 184328 | tf_op jit(solution)/shard_map/ppermute | solution.py:20
  85.1 46.2 %collective-permute-start.2 = (f32[2,5,10,1,512]{4,0,3,2,1:T(2,128)}, f32[2,5,10,1,512]{4,0,3,2,1:T(2,128)}, u32[]{:S(2)}, u32[]{:S(2)}) collective-permute-start(f32[2,5,10,1,512]{4,0,3,2,1:T(2,128)} %get-tuple-element.19), channel_id=1, source_target_pairs={{1,0},{3,2},{5,4},{7,6},{9,8},{11,10},{13,12},{15,14},{17,16},{19,... | collective-permute-start | bytes 614408 | tf_op jit(solution)/shard_map/ppermute | solution.py:21
  92.5 38.9 %collective-permute-start.3 = (f32[2,5,10,1,512]{4,0,3,2,1:T(2,128)}, f32[2,5,10,1,512]{4,0,3,2,1:T(2,128)}, u32[]{:S(2)}, u32[]{:S(2)}) collective-permute-start(f32[2,5,10,1,512]{4,0,3,2,1:T(2,128)} %get-tuple-element.20), channel_id=1, source_target_pairs={{0,1},{2,3},{4,5},{6,7},{8,9},{10,11},{12,13},{14,15},{16,17},{18,... | collective-permute-start | bytes 614408 | tf_op jit(solution)/shard_map/ppermute | solution.py:20
  174.1 8.6 %collective-permute-start.4 = (f32[2,5,1,16,512]{4,0,3,2,1:T(2,128)S(1)}, f32[2,5,1,16,512]{4,0,3,2,1:T(2,128)S(1)}, u32[]{:S(2)}, u32[]{:S(2)}) collective-permute-start(f32[2,5,1,16,512]{4,0,3,2,1:T(2,128)S(1)} %get-tuple-element.52), channel_id=1, source_target_pairs={{8,0},{16,8},{24,16},{32,24},{40,32},{48,40},{56,48},{64,56},{72,6... | collective-permute-start | bytes 983048 | tf_op jit(solution)/shard_map/ppermute | solution.py:21
  176.2 10.7 %collective-permute-start.5 = (f32[2,5,1,16,512]{4,0,3,2,1:T(2,128)S(1)}, f32[2,5,1,16,512]{4,0,3,2,1:T(2,128)S(1)}, u32[]{:S(2)}, u32[]{:S(2)}) collective-permute-start(f32[2,5,1,16,512]{4,0,3,2,1:T(2,128)S(1)} %get-tuple-element.51), channel_id=1, source_target_pairs={{0,8},{8,16},{16,24},{24,32},{32,40},{40,48},{48,56},{56,64},{64,7... | collective-permute-start | bytes 983048 | tf_op jit(solution)/shard_map/ppermute | solution.py:20
  182.7 16.9 %copy-start.3 = (f32[8,16,512]{2,1,0:T(8,128)S(1)}, f32[8,16,512]{2,1,0:T(8,128)}, u32[]{:S(2)}) copy-start(f32[8,16,512]{2,1,0:T(8,128)} %get-tuple-element.74) | copy-start | bytes 786436
  182.7 16.8 %copy-start.16 = (pred[512]{0:T(512)(128)(4,1)S(1)}, pred[512]{0:T(512)(128)(4,1)}, u32[]{:S(2)}) copy-start(pred[512]{0:T(512)(128)(4,1)} %get-tuple-element.85) | copy-start | bytes 1540
  187.1 6.4 %collective-permute-start.6 = (f32[2,5,10,1,512]{4,0,3,2,1:T(2,128)S(1)}, f32[2,5,10,1,512]{4,0,3,2,1:T(2,128)S(1)}, u32[]{:S(2)}, u32[]{:S(2)}) collective-permute-start(f32[2,5,10,1,512]{4,0,3,2,1:T(2,128)S(1)} %get-tuple-element.17), channel_id=1, source_target_pairs={{1,0},{3,2},{5,4},{7,6},{9,8},{11,10},{13,12},{15,14},{17,16},{19,... | collective-permute-start | bytes 614408 | tf_op jit(solution)/shard_map/ppermute | solution.py:21
  190.3 9.2 %collective-permute-start.7 = (f32[2,5,10,1,512]{4,0,3,2,1:T(2,128)S(1)}, f32[2,5,10,1,512]{4,0,3,2,1:T(2,128)S(1)}, u32[]{:S(2)}, u32[]{:S(2)}) collective-permute-start(f32[2,5,10,1,512]{4,0,3,2,1:T(2,128)S(1)} %get-tuple-element.18), channel_id=1, source_target_pairs={{0,1},{2,3},{4,5},{6,7},{8,9},{10,11},{12,13},{14,15},{16,17},{18,... | collective-permute-start | bytes 614408 | tf_op jit(solution)/shard_map/ppermute | solution.py:20
  219.9 10.0 %collective-permute-start.8 = (f32[2,5,1,16,512]{4,0,3,2,1:T(2,128)S(1)}, f32[2,5,1,16,512]{4,0,3,2,1:T(2,128)S(1)}, u32[]{:S(2)}, u32[]{:S(2)}) collective-permute-start(f32[2,5,1,16,512]{4,0,3,2,1:T(2,128)S(1)} %get-tuple-element.46), channel_id=1, source_target_pairs={{8,0},{16,8},{24,16},{32,24},{40,32},{48,40},{56,48},{64,56},{72,6... | collective-permute-start | bytes 983048 | tf_op jit(solution)/shard_map/ppermute | solution.py:21
  221.8 8.7 %collective-permute-start.9 = (f32[2,5,1,16,512]{4,0,3,2,1:T(2,128)S(1)}, f32[2,5,1,16,512]{4,0,3,2,1:T(2,128)S(1)}, u32[]{:S(2)}, u32[]{:S(2)}) collective-permute-start(f32[2,5,1,16,512]{4,0,3,2,1:T(2,128)S(1)} %get-tuple-element.45), channel_id=1, source_target_pairs={{0,8},{8,16},{16,24},{24,32},{32,40},{40,48},{48,56},{56,64},{64,7... | collective-permute-start | bytes 983048 | tf_op jit(solution)/shard_map/ppermute | solution.py:20
  228.4 13.5 %copy-start.2 = (f32[8,16,512]{2,1,0:T(8,128)S(1)}, f32[8,16,512]{2,1,0:T(8,128)}, u32[]{:S(2)}) copy-start(f32[8,16,512]{2,1,0:T(8,128)} %get-tuple-element.73) | copy-start | bytes 786436
  230.7 5.3 collective-permute-start.10
  232.8 9.2 %collective-permute-start.11 = (f32[2,5,10,1,512]{4,0,3,2,1:T(2,128)S(1)}, f32[2,5,10,1,512]{4,0,3,2,1:T(2,128)S(1)}, u32[]{:S(2)}, u32[]{:S(2)}) collective-permute-start(f32[2,5,10,1,512]{4,0,3,2,1:T(2,128)S(1)} %get-tuple-element.16), channel_id=1, source_target_pairs={{0,1},{2,3},{4,5},{6,7},{8,9},{10,11},{12,13},{14,15},{16,17},{18,... | collective-permute-start | bytes 614408 | tf_op jit(solution)/shard_map/ppermute | solution.py:20
  262.1 12.3 %collective-permute-start.12 = (f32[2,5,1,16,512]{4,0,3,2,1:T(2,128)S(1)}, f32[2,5,1,16,512]{4,0,3,2,1:T(2,128)S(1)}, u32[]{:S(2)}, u32[]{:S(2)}) collective-permute-start(f32[2,5,1,16,512]{4,0,3,2,1:T(2,128)S(1)} %get-tuple-element.40), channel_id=1, source_target_pairs={{8,0},{16,8},{24,16},{32,24},{40,32},{48,40},{56,48},{64,56},{72,6... | collective-permute-start | bytes 983048 | tf_op jit(solution)/shard_map/ppermute | solution.py:21
  265.7 8.7 %collective-permute-start.13 = (f32[2,5,1,16,512]{4,0,3,2,1:T(2,128)S(1)}, f32[2,5,1,16,512]{4,0,3,2,1:T(2,128)S(1)}, u32[]{:S(2)}, u32[]{:S(2)}) collective-permute-start(f32[2,5,1,16,512]{4,0,3,2,1:T(2,128)S(1)} %get-tuple-element.39), channel_id=1, source_target_pairs={{0,8},{8,16},{16,24},{24,32},{32,40},{40,48},{48,56},{56,64},{64,7... | collective-permute-start | bytes 983048 | tf_op jit(solution)/shard_map/ppermute | solution.py:20
  271.7 13.8 %copy-start.7 = (f32[8,16,512]{2,1,0:T(8,128)S(1)}, f32[8,16,512]{2,1,0:T(8,128)}, u32[]{:S(2)}) copy-start(f32[8,16,512]{2,1,0:T(8,128)} %get-tuple-element.75) | copy-start | bytes 786436
  274.6 5.0 collective-permute-start.14
  276.4 9.2 %collective-permute-start.15 = (f32[2,5,10,1,512]{4,0,3,2,1:T(2,128)S(1)}, f32[2,5,10,1,512]{4,0,3,2,1:T(2,128)S(1)}, u32[]{:S(2)}, u32[]{:S(2)}) collective-permute-start(f32[2,5,10,1,512]{4,0,3,2,1:T(2,128)S(1)} %get-tuple-element.14), channel_id=1, source_target_pairs={{0,1},{2,3},{4,5},{6,7},{8,9},{10,11},{12,13},{14,15},{16,17},{18,... | collective-permute-start | bytes 614408 | tf_op jit(solution)/shard_map/ppermute | solution.py:20
  304.5 13.5 %collective-permute-start.16 = (f32[2,5,1,16,512]{4,0,3,2,1:T(2,128)S(1)}, f32[2,5,1,16,512]{4,0,3,2,1:T(2,128)S(1)}, u32[]{:S(2)}, u32[]{:S(2)}) collective-permute-start(f32[2,5,1,16,512]{4,0,3,2,1:T(2,128)S(1)} %get-tuple-element.34), channel_id=1, source_target_pairs={{8,0},{16,8},{24,16},{32,24},{40,32},{48,40},{56,48},{64,56},{72,6... | collective-permute-start | bytes 983048 | tf_op jit(solution)/shard_map/ppermute | solution.py:21
  309.1 8.9 %collective-permute-start.17 = (f32[2,5,1,16,512]{4,0,3,2,1:T(2,128)S(1)}, f32[2,5,1,16,512]{4,0,3,2,1:T(2,128)S(1)}, u32[]{:S(2)}, u32[]{:S(2)}) collective-permute-start(f32[2,5,1,16,512]{4,0,3,2,1:T(2,128)S(1)} %get-tuple-element.33), channel_id=1, source_target_pairs={{0,8},{8,16},{16,24},{24,32},{32,40},{40,48},{48,56},{56,64},{64,7... | collective-permute-start | bytes 983048 | tf_op jit(solution)/shard_map/ppermute | solution.py:20
  318.2 4.9 collective-permute-start.18
  319.9 9.2 %collective-permute-start.19 = (f32[2,5,10,1,512]{4,0,3,2,1:T(2,128)S(1)}, f32[2,5,10,1,512]{4,0,3,2,1:T(2,128)S(1)}, u32[]{:S(2)}, u32[]{:S(2)}) collective-permute-start(f32[2,5,10,1,512]{4,0,3,2,1:T(2,128)S(1)} %get-tuple-element.12), channel_id=1, source_target_pairs={{0,1},{2,3},{4,5},{6,7},{8,9},{10,11},{12,13},{14,15},{16,17},{18,... | collective-permute-start | bytes 614408 | tf_op jit(solution)/shard_map/ppermute | solution.py:20
  349.1 13.0 %collective-permute-start.20 = (f32[2,5,1,16,512]{4,0,3,2,1:T(2,128)S(1)}, f32[2,5,1,16,512]{4,0,3,2,1:T(2,128)S(1)}, u32[]{:S(2)}, u32[]{:S(2)}) collective-permute-start(f32[2,5,1,16,512]{4,0,3,2,1:T(2,128)S(1)} %get-tuple-element.28), channel_id=1, source_target_pairs={{8,0},{16,8},{24,16},{32,24},{40,32},{48,40},{56,48},{64,56},{72,6... | collective-permute-start | bytes 983048 | tf_op jit(solution)/shard_map/ppermute | solution.py:21
  353.2 8.9 %collective-permute-start.21 = (f32[2,5,1,16,512]{4,0,3,2,1:T(2,128)S(1)}, f32[2,5,1,16,512]{4,0,3,2,1:T(2,128)S(1)}, u32[]{:S(2)}, u32[]{:S(2)}) collective-permute-start(f32[2,5,1,16,512]{4,0,3,2,1:T(2,128)S(1)} %get-tuple-element.27), channel_id=1, source_target_pairs={{0,8},{8,16},{16,24},{24,32},{32,40},{40,48},{48,56},{56,64},{64,7... | collective-permute-start | bytes 983048 | tf_op jit(solution)/shard_map/ppermute | solution.py:20
  362.4 5.1 collective-permute-start.22
  364.2 9.2 %collective-permute-start.23 = (f32[2,5,10,1,512]{4,0,3,2,1:T(2,128)S(1)}, f32[2,5,10,1,512]{4,0,3,2,1:T(2,128)S(1)}, u32[]{:S(2)}, u32[]{:S(2)}) collective-permute-start(f32[2,5,10,1,512]{4,0,3,2,1:T(2,128)S(1)} %get-tuple-element.10), channel_id=1, source_target_pairs={{0,1},{2,3},{4,5},{6,7},{8,9},{10,11},{12,13},{14,15},{16,17},{18,... | collective-permute-start | bytes 614408 | tf_op jit(solution)/shard_map/ppermute | solution.py:20
  393.3 12.8 %collective-permute-start.24 = (f32[2,5,1,16,512]{4,0,3,2,1:T(2,128)S(1)}, f32[2,5,1,16,512]{4,0,3,2,1:T(2,128)S(1)}, u32[]{:S(2)}, u32[]{:S(2)}) collective-permute-start(f32[2,5,1,16,512]{4,0,3,2,1:T(2,128)S(1)} %get-tuple-element.26), channel_id=1, source_target_pairs={{8,0},{16,8},{24,16},{32,24},{40,32},{48,40},{56,48},{64,56},{72,6... | collective-permute-start | bytes 983048 | tf_op jit(solution)/shard_map/ppermute | solution.py:21
  397.2 8.9 %collective-permute-start.25 = (f32[2,5,1,16,512]{4,0,3,2,1:T(2,128)S(1)}, f32[2,5,1,16,512]{4,0,3,2,1:T(2,128)S(1)}, u32[]{:S(2)}, u32[]{:S(2)}) collective-permute-start(f32[2,5,1,16,512]{4,0,3,2,1:T(2,128)S(1)} %get-tuple-element.25), channel_id=1, source_target_pairs={{0,8},{8,16},{16,24},{24,32},{32,40},{40,48},{48,56},{56,64},{64,7... | collective-permute-start | bytes 983048 | tf_op jit(solution)/shard_map/ppermute | solution.py:20
  406.3 5.1 collective-permute-start.26
  408.2 9.2 %collective-permute-start.27 = (f32[2,5,10,1,512]{4,0,3,2,1:T(2,128)S(1)}, f32[2,5,10,1,512]{4,0,3,2,1:T(2,128)S(1)}, u32[]{:S(2)}, u32[]{:S(2)}) collective-permute-start(f32[2,5,10,1,512]{4,0,3,2,1:T(2,128)S(1)} %get-tuple-element.8), channel_id=1, source_target_pairs={{0,1},{2,3},{4,5},{6,7},{8,9},{10,11},{12,13},{14,15},{16,17},{18,... | collective-permute-start | bytes 614408 | tf_op jit(solution)/shard_map/ppermute | solution.py:20
  520.3 20.8 %copy-start.8 = (f32[2,5,4,8,256]{4,1,3,2,0:T(8,128)S(1)}, f32[2,5,4,8,256]{4,1,3,2,0:T(8,128)}, u32[]{:S(2)}) copy-start(f32[2,5,4,8,256]{4,1,3,2,0:T(8,128)} %copy.116) | copy-start | bytes 983044
  520.3 20.8 %copy-start.13 = (f32[4,8,256]{2,1,0:T(8,128)S(1)}, f32[4,8,256]{2,1,0:T(8,128)}, u32[]{:S(2)}) copy-start(f32[4,8,256]{2,1,0:T(8,128)} %get-tuple-element.77) | copy-start | bytes 98308
  520.4 6.6 %collective-permute-start.32 = (f32[2,5,1,8,256]{4,1,3,2,0:T(8,128)S(1)}, f32[2,5,1,8,256]{4,1,3,2,0:T(8,128)S(1)}, u32[]{:S(2)}, u32[]{:S(2)}) collective-permute-start(f32[2,5,1,8,256]{4,1,3,2,0:T(8,128)S(1)} %get-tuple-element.72), channel_id=1, source_target_pairs={{8,0},{16,8},{24,16},{32,24},{40,32},{48,40},{56,48},{64,56},{72,6... | collective-permute-start | bytes 245768 | tf_op jit(solution)/shard_map/ppermute | solution.py:21
  524.4 6.3 %collective-permute-start.33 = (f32[2,5,1,8,256]{4,1,3,2,0:T(8,128)S(1)}, f32[2,5,1,8,256]{4,1,3,2,0:T(8,128)S(1)}, u32[]{:S(2)}, u32[]{:S(2)}) collective-permute-start(f32[2,5,1,8,256]{4,1,3,2,0:T(8,128)S(1)} %get-tuple-element.71), channel_id=1, source_target_pairs={{0,8},{8,16},{16,24},{24,32},{32,40},{40,48},{48,56},{56,64},{64,7... | collective-permute-start | bytes 245768 | tf_op jit(solution)/shard_map/ppermute | solution.py:20
  530.7 4.6 collective-permute-start.34
  533.1 8.0 %collective-permute-start.35 = (f32[2,5,6,1,256]{4,1,3,2,0:T(8,128)S(1)}, f32[2,5,6,1,256]{4,1,3,2,0:T(8,128)S(1)}, u32[]{:S(2)}, u32[]{:S(2)}) collective-permute-start(f32[2,5,6,1,256]{4,1,3,2,0:T(8,128)S(1)} %get-tuple-element.64), channel_id=1, source_target_pairs={{0,1},{2,3},{4,5},{6,7},{8,9},{10,11},{12,13},{14,15},{16,17},{18,... | collective-permute-start | bytes 184328 | tf_op jit(solution)/shard_map/ppermute | solution.py:20
  (8 other events, 42.7 us)
Sparse Core Ops, SparseCore 0:
  9.0 102.0 all-gather.1
where the time goes:
time: 631 us; the launch traced here: 625 us
  local copies, waits for them, and re-layouts  206 us (33%)
  other arithmetic  148 us (23%)
  starting transfers between devices  87.6 us (14%)
  waiting for transfers between devices  87 us (14%)
  matrix products  80.8 us (13%)
  between operations  14.5 us (2%)
    add x5, other arithmetic, shards(): begin + weight * step * residual_of(field, source, low_ghost, high_ghost,...  70.6 us
    ppermute x18, starting transfers between devices, with_halo(): after = lax.ppermute(leading, axis, down)  53.7 us
    ppermute x18, waiting for transfers between devices, with_halo(): before = lax.ppermute(last, axis, up)  49.9 us
    reduce_sum x1, other arithmetic, shards(): last.reshape(inst_dev, comps, half_x, 2, half_z, 2, half_y, 2)  47 us
    dot_general x7, matrix products, residual_of(): mixed = jnp.einsum('cd,ndxzy->ncxzy', coupling, field, precision=HIGH)  39.8 us
    reshape x1, local copies, waits for them, and re-layouts, shards(): return field + fine_corr.reshape(inst_dev, comps, cells_x, cells_z, cells_y)  39.5 us
    slice x12, local copies, waits for them, and re-layouts, residual_of(): jnp.roll(field, -1, axis=4)  37.4 us
    dot_general x1, matrix products, shards(): source = jnp.einsum('nk,kcxzy->ncxzy', rows, piece, precision=HIGH)  37 us
  transfers between devices with their start and end apart: 37, of which 24 were waited for; matrix products, arithmetic and copies ran while one was open for 57% of the time, Pallas kernels for 0%

commit v1 on v0

v1 whole, which is shorter than its diff:
```python
import functools
import math

import jax
import jax.numpy as jnp
import numpy as np
from jax import lax
from jax.experimental import pallas as pl
from jax.experimental.pallas import tpu as pltpu
from jax.sharding import PartitionSpec as P

MESH = pl.DeviceIdType.MESH
WEIGHTS = (0.25, 0.5, 1.0)
STAGES = 6
NEAR = 12
LOOKAHEAD = 2


def spectral(d):
    if d == 0:
        return 0.0
    return float(0.5 * (-1.0) ** abs(d) * math.cos(math.pi * d / 8) / math.sin(math.pi * d / 8))


D1, D2, D3, D4 = spectral(1), spectral(2), spectral(3), spectral(4)


def leg_kernel(
    forcing, start, kappa, coupling, lag, out_u, out_e,
    S, A, B, F, R1, C2, R2, K, W, E, EG, GP, RHS, WC, E1, E2,
    ld_s, ld_f, ld_k, p1s, p1r, p2s, p2r, es, er, xs_s, xs_r, zs_s, zs_r, cx_s, cx_r, cz_s, cz_r, out_sem,
):
    comps = 5
    sp, it, co = lax.axis_index("space"), lax.axis_index("instance"), lax.axis_index("coarse")
    spaces = lax.axis_size("space")
    odd = lax.rem(it, 2)
    pa = lax.rem(it + 1 + 2 * odd, 4)
    pb = lax.rem(it + 3 + 2 * odd, 4)
    has_lo, has_hi = sp > 0, sp < spaces - 1

    sub = lax.broadcasted_iota(jnp.int32, (8, 128), 0)
    lane = lax.broadcasted_iota(jnp.int32, (8, 128), 1)
    inst = sub // 4
    quarter = sub % 4

    sign = 2 * co - 1
    base = 15 * (1 - co)

    def zcell(d):
        return base + sign * d

    def zrange(d0, d1):
        return (1 - co) * (16 - d1) + co * d0

    order = (0, 7, 1, 6, 2, 5, 3, 4)
    for x in order:
        for n in range(2):
            for q in range(4):
                pltpu.make_async_copy(
                    start.at[n, :, x, :, pl.ds(q * 128, 128)],
                    S.at[x + 1, :, pl.ds(1, 16), n * 4 + q, :], ld_s.at[x],
                ).start()
    for n in range(2):
        for q in range(4):
            pltpu.make_async_copy(
                kappa.at[:, :, pl.ds(q * 128, 128)], K.at[:, :, n * 4 + q, :], ld_k.at[0]
            ).start()
    for x in order:
        for n in range(2):
            for q in range(4):
                pltpu.make_async_copy(
                    forcing.at[n, :, x, :, pl.ds(q * 128, 128)],
                    F.at[x, :, :, n * 4 + q, :], ld_f.at[x],
                ).start()

    zero16 = jnp.zeros((comps, 16, 8, 128), jnp.float32)
    zero1 = jnp.zeros((comps, 8, 128), jnp.float32)
    zero8 = jnp.zeros((comps, 8, 8, 128), jnp.float32)
    zend = 17 * co
    zend_c = 9 * co

    for x in range(8):
        for buf in (S, A, B):
            buf[x + 1, :, zend] = zero1
    for x in range(4):
        E1[x + 1, :, zend_c] = zero1

    @pl.when(sp == 0)
    def _():
        for buf in (S, A, B):
            buf[0, :, pl.ds(1, 16)] = zero16
        E1[0, :, pl.ds(1, 8)] = zero8

    @pl.when(sp == spaces - 1)
    def _():
        for buf in (S, A, B):
            buf[9, :, pl.ds(1, 16)] = zero16
        E1[5, :, pl.ds(1, 8)] = zero8

    bar = pltpu.get_barrier_semaphore()
    for r in (1, 2, 3):
        pl.semaphore_signal(bar, inc=1, device_id={"instance": lax.rem(it + r, 4)}, device_id_type=MESH)
    pl.semaphore_signal(bar, inc=1, device_id={"coarse": 1 - co}, device_id_type=MESH)

    @pl.when(has_lo)
    def _():
        pl.semaphore_signal(bar, inc=1, device_id={"space": sp - 1}, device_id_type=MESH)

    @pl.when(has_hi)
    def _():
        pl.semaphore_signal(bar, inc=1, device_id={"space": sp + 1}, device_id_type=MESH)

    pl.semaphore_wait(bar, 4 + has_lo.astype(jnp.int32) + has_hi.astype(jnp.int32))

    halves = ((0, NEAR), (NEAR, 16))

    def level_buf(level):
        return (S, A, B)[level % 3]

    def level_range(level, h):
        cut = NEAR - max(level - 1, 0)
        return (0, cut) if h == 0 else (cut, 16)

    def xface(level, h, side):
        buf = level_buf(level)
        d0, d1 = level_range(level, h)
        z0 = 1 + zrange(d0, d1)
        i = ((level % 3) * 2 + h) * 2 + side
        src = buf.at[1 if side == 0 else 8, :, pl.ds(z0, d1 - d0)]
        dst = buf.at[9 if side == 0 else 0, :, pl.ds(z0, d1 - d0)]
        return pltpu.make_async_remote_copy(
            src, dst, xs_s.at[i], xs_r.at[i],
            device_id={"space": sp - 1 if side == 0 else sp + 1}, device_id_type=MESH,
        )

    def x_send(level, h):
        pl.when(has_lo)(lambda: xface(level, h, 0).start())
        pl.when(has_hi)(lambda: xface(level, h, 1).start())

    def x_sent(level, h):
        pl.when(has_lo)(lambda: xface(level, h, 0).wait_send())
        pl.when(has_hi)(lambda: xface(level, h, 1).wait_send())

    def x_recv(level, h):
        pl.when(has_hi)(lambda: xface(level, h, 0).wait_recv())
        pl.when(has_lo)(lambda: xface(level, h, 1).wait_recv())

    def zface(level, x):
        buf = level_buf(level)
        i = (level % 3) * 8 + x
        return pltpu.make_async_remote_copy(
            buf.at[x + 1, :, pl.ds(1 + base, 1)], buf.at[x + 1, :, pl.ds(17 * co_other(), 1)],
            zs_s.at[i], zs_r.at[i], device_id={"coarse": 1 - co}, device_id_type=MESH,
        )

    def co_other():
        return co

    def raw(q, x, partner):
        h, t = divmod(q, 4)
        d0, d1 = halves[h]
        z0 = zrange(d0, d1)
        i = q * 2 + (0 if x < 4 else 1)
        return pltpu.make_async_remote_copy(
            S.at[x + 1, :, pl.ds(1 + z0, d1 - d0)], R1.at[x, :, pl.ds(z0, d1 - d0)],
            p1s.at[i], p1r.at[i], device_id={"instance": partner}, device_id_type=MESH,
        )

    def sums(q, x, partner):
        h, t = divmod(q, 4)
        d0, d1 = halves[h]
        z0 = zrange(d0, d1)
        i = q * 2 + (0 if x < 4 else 1)
        return pltpu.make_async_remote_copy(
            C2.at[x, :, pl.ds(z0, d1 - d0)], R2.at[x, :, pl.ds(z0, d1 - d0)],
            p2s.at[i], p2r.at[i], device_id={"instance": partner}, device_id_type=MESH,
        )

    def planes(q):
        t = q % 4
        return ((t, pa, pb), (7 - t, pb, pa))

    def raw_start(q):
        for x, first, second in planes(q):
            raw(q, x, first).start()

    def wait_state(x):
        view = S.at[x + 1, :, pl.ds(1, 16)]
        pltpu.make_async_copy(view, view, ld_s.at[x]).wait()

    for x in order:
        wait_state(x)
        if x >= 4 and 7 - x < LOOKAHEAD:
            raw_start(7 - x)
    x_send(0, 0)
    x_send(0, 1)
    for x in order:
        zface(0, x).start()

    def pack(z, carry):
        for xh in range(2):
            for xq in range(4):
                spot = xq * 32 + 2 * z
                mine = (lane // 2) == xq * 16 + z
                for c in range(comps):
                    v = pltpu.roll(S[xh * 4 + xq + 1, c, z + 1], spot + 1, 1)
                    E[c, xh] = jnp.where(mine, v, E[c, xh])
        return carry

    E[...] = jnp.zeros_like(E)
    lax.fori_loop(0, 16, pack, 0)

    def edge(r):
        return pltpu.make_async_remote_copy(
            E, EG.at[r - 1], es.at[r - 1], er.at[r - 1],
            device_id={"instance": lax.rem(it + r, 4)}, device_id_type=MESH,
        )

    for r in (1, 2, 3):
        edge(r).start()

    pltpu.make_async_copy(K, K, ld_k.at[0]).wait()
    even_lane = lane % 2 == 0

    def pair_sum(v):
        return v + jnp.where(even_lane, pltpu.roll(v, 127, 1), pltpu.roll(v, 1, 1))

    def steps(zc, carry):
        for xc in range(4):
            total = None
            for dx in range(2):
                for dz in range(2):
                    k = K[2 * xc + dx, 2 * zc + dz]
                    W[2 * xc + dx, 2 * zc + dz] = 0.8 / (6.0 + k)
                    total = k if total is None else total + k
            WC[xc, zc] = 0.8 / (6.0 + pair_sum(total) * 0.125)
        return carry

    lax.fori_loop(0, 8, steps, 0)

    for x in order:
        view = F.at[x]
        pltpu.make_async_copy(view, view, ld_f.at[x]).wait()

    def ghosts():
        zl = (lane % 32) // 2
        lags = jnp.zeros((8, 128), jnp.int32)
        for z in range(16):
            lags = jnp.where(zl == z, lag[z], lags)
        mine = 2 * it + inst
        low = (mine - lags + 8) % 8
        high = (mine + lags) % 8
        want = jnp.where(
            (quarter == 0) & (lane % 2 == 1), low, jnp.where((quarter == 3) & (lane % 2 == 0), high, -1)
        )
        low_slot = lane % 2 == 1
        for r in (1, 2, 3):
            edge(r).wait_recv()
        for c in range(comps):
            for xh in range(2):
                total = jnp.zeros((8, 128), jnp.float32)
                for r in range(4):
                    p = E[c, xh] if r == 0 else EG[r - 1, c, xh]
                    who = lax.rem(it + 4 - r, 4)
                    up, down = pltpu.roll(p, 1, 1), pltpu.roll(p, 127, 1)
                    same = jnp.where(low_slot, pltpu.roll(up, 5, 0), pltpu.roll(down, 3, 0))
                    other = jnp.where(low_slot, pltpu.roll(up, 1, 0), pltpu.roll(down, 7, 0))
                    total = jnp.where(want == 2 * who + inst, same, total)
                    total = jnp.where(want == 2 * who + 1 - inst, other, total)
                GP[c, xh] = total

        ends = ((lane == 0) & (quarter == 0)) | ((lane == 127) & (quarter == 3))

        def unpack(z, carry):
            for xh in range(2):
                for xq in range(4):
                    back = 127 - xq * 32 - 2 * z
                    for c in range(comps):
                        v = pltpu.roll(GP[c, xh], back, 1)
                        x = xh * 4 + xq
                        F[x, c, z] = F[x, c, z] + jnp.where(ends, v, 0.0)
            return carry

        lax.fori_loop(0, 16, unpack, 0)

    def by_inst(v0, v1):
        return jnp.where(inst == 0, v0, v1).astype(jnp.float32)

    delta = by_inst(-D1, D1)
    gamma = by_inst(D3, -D3)
    plus = by_inst(D1, D3)
    minus = by_inst(-D3, -D1)

    def source_part(q):
        h, t = divmod(q, 4)
        d0, d1 = halves[h]
        z0 = zrange(d0, d1)
        for x, first, second in planes(q):
            raw(q, x, first).wait_recv()
        for x, first, second in planes(q):
            up = odd == (1 if x < 4 else 0)
            alpha = jnp.where(up, D2, -D2).astype(jnp.float32)
            beta = jnp.where(up, plus, minus)

            def part(i, carry):
                z = z0 + i
                for c in range(comps):
                    u, v = S[x + 1, c, z + 1], R1[x, c, z]
                    ur, vr = pltpu.roll(u, 4, 0), pltpu.roll(v, 4, 0)
                    C2[x, c, z] = alpha * u + beta * ur + D4 * v + gamma * vr
                    F[x, c, z] = F[x, c, z] - (delta * ur + alpha * v + beta * vr)
                return carry

            lax.fori_loop(0, d1 - d0, part, 0)
            sums(q, x, second).start()

    def source_rest(q):
        h, t = divmod(q, 4)
        d0, d1 = halves[h]
        z0 = zrange(d0, d1)
        for x, first, second in planes(q):
            sums(q, x, second).wait_recv()
            raw(q, x, first).wait_send()

        def rest(i, carry):
            z = z0 + i
            for x, first, second in planes(q):
                for c in range(comps):
                    F[x, c, z] = F[x, c, z] - R2[x, c, z]
            return carry

        lax.fori_loop(0, d1 - d0, rest, 0)

    lane_lo, lane_hi = lane == 0, lane == 127
    fix_lo = lane_lo & (quarter != 0)
    fix_hi = lane_hi & (quarter != 3)
    zero = jnp.zeros((8, 128), jnp.float32)

    def beside_y(u):
        lo, hi = pltpu.roll(u, 1, 1), pltpu.roll(u, 127, 1)
        lower = jnp.where(fix_lo, pltpu.roll(lo, 1, 0), jnp.where(lane_lo, zero, lo))
        upper = jnp.where(fix_hi, pltpu.roll(hi, 7, 0), jnp.where(lane_hi, zero, hi))
        return lower + upper

    def mix(us, c):
        total = coupling[c, 0] * us[0]
        for d in range(1, comps):
            total = total + coupling[c, d] * us[d]
        return total

    def balance(src, x, z, us):
        got = []
        for c in range(comps):
            near = (src[x, c, z + 1] + src[x + 2, c, z + 1]) + (src[x + 1, c, z] + src[x + 1, c, z + 2])
            got.append((F[x, c, z] + near) + (beside_y(us[c]) - mix(us, c)))
        return got

    def stage_block(k, j, h):
        src, dst = level_buf(k - 1), level_buf(k)
        d0, d1 = level_range(k, h)
        weight = WEIGHTS[(k - 1) % 3]
        begin = S

        def body(d, carry):
            z = zcell(d)
            for x in (j, 7 - j):
                us = [src[x + 1, c, z + 1] for c in range(comps)]
                bal = balance(src, x, z, us)
                w = W[x, z] * weight
                for c in range(comps):
                    own = us[c] if (k - 1) % 3 == 0 else begin[x + 1, c, z + 1]
                    dst[x + 1, c, z + 1] = (own - (0.8 * weight) * us[c]) + w * bal[c]
            return carry

        lax.fori_loop(d0, d1, body, 0)

    def last_block(j, h):
        d0, d1 = level_range(7, h)

        def body(m, carry):
            zc = (1 - co) * (7 - m) + co * m
            for x in (j, 7 - j):
                total = [None] * comps
                for dz in range(2):
                    z = 2 * zc + dz
                    us = [S[x + 1, c, z + 1] for c in range(comps)]
                    bal = balance(S, x, z, us)
                    diag = 6.0 + K[x, z]
                    for c in range(comps):
                        res = bal[c] - diag * us[c]
                        total[c] = res if total[c] is None else total[c] + res
                for c in range(comps):
                    if j % 2 == 0:
                        RHS[x // 2, c, zc] = total[c]
                    else:
                        RHS[x // 2, c, zc] = RHS[x // 2, c, zc] + total[c]
            return carry

        lax.fori_loop(d0 // 2, d1 // 2, body, 0)

    def run(k, j, h):
        if j == 0:
            x_recv(k - 1, h)
            if 3 <= k <= STAGES:
                x_sent(k - 3, h)
        if h == 0:
            for x in (j, 7 - j):
                zface(k - 1, x).wait_recv()
                if 3 <= k <= STAGES:
                    zface(k - 3, x).wait_send()
        if k <= STAGES:
            stage_block(k, j, h)
            if j == 0:
                x_send(k, h)
            if h == 0:
                for x in (j, 7 - j):
                    zface(k, x).start()
            if k == STAGES and h == 1:
                for x in (j, 7 - j):
                    u_out(x).start()
        else:
            last_block(j, h)

    def u_out(x):
        return pltpu.make_async_copy(S.at[x + 1, :, pl.ds(1, 16)], out_u.at[x], out_sem.at[x])

    def wave(t, h):
        for k in range(1, STAGES + 2):
            j = t - k + 1
            if 0 <= j <= 3:
                run(k, j, h)

    def first_sweep(xc):
        def body(zc, carry):
            for c in range(comps):
                E1[xc + 1, c, zc + 1] = WC[xc, zc] * pair_sum(RHS[xc, c, zc])
            return carry

        lax.fori_loop(0, 8, body, 0)

    def cx(side):
        return pltpu.make_async_remote_copy(
            E1.at[1 if side == 0 else 4, :, pl.ds(1, 8)], E1.at[5 if side == 0 else 0, :, pl.ds(1, 8)],
            cx_s.at[side], cx_r.at[side],
            device_id={"space": sp - 1 if side == 0 else sp + 1}, device_id_type=MESH,
        )

    def cz(xc):
        return pltpu.make_async_remote_copy(
            E1.at[xc + 1, :, pl.ds(1 + 7 * (1 - co), 1)], E1.at[xc + 1, :, pl.ds(9 * co, 1)],
            cz_s.at[xc], cz_r.at[xc], device_id={"coarse": 1 - co}, device_id_type=MESH,
        )

    lo2, hi2 = lane < 2, lane >= 126
    first_q, last_q = quarter == 0, quarter == 3

    def beside_y2(u):
        lo, hi = pltpu.roll(u, 2, 1), pltpu.roll(u, 126, 1)
        wrap_lo = jnp.where(first_q, pltpu.roll(lo, 5, 0), pltpu.roll(lo, 1, 0))
        wrap_hi = jnp.where(last_q, pltpu.roll(hi, 3, 0), pltpu.roll(hi, 7, 0))
        return jnp.where(lo2, wrap_lo, lo) + jnp.where(hi2, wrap_hi, hi)

    def second_sweep(xc):
        def body(zc, carry):
            es_ = [E1[xc + 1, c, zc + 1] for c in range(comps)]
            w = WC[xc, zc]
            for c in range(comps):
                near = (E1[xc, c, zc + 1] + E1[xc + 2, c, zc + 1]) + (E1[xc + 1, c, zc] + E1[xc + 1, c, zc + 2])
                E2[xc, c, zc] = 1.2 * es_[c] + w * ((near + beside_y2(es_[c])) - mix(es_, c))
            return carry

        lax.fori_loop(0, 8, body, 0)

    for q in range(8):
        source_part(q)
        if q + LOOKAHEAD < 8:
            raw_start(q + LOOKAHEAD)
        if q == 0:
            ghosts()
        if q >= 1:
            source_rest(q - 1)
            if q <= 4:
                wave(q - 1, 0)
            else:
                wave(q - 5, 1)
                if q == 6:
                    wave(4, 0)
    source_rest(7)
    wave(3, 1)
    wave(5, 0)
    wave(6, 0)
    wave(4, 1)
    wave(7, 0)
    wave(5, 1)
    wave(8, 0)
    wave(9, 0)
    wave(6, 1)
    wave(7, 1)
    first_sweep(0)
    first_sweep(3)
    pl.when(has_lo)(lambda: cx(0).start())
    pl.when(has_hi)(lambda: cx(1).start())
    cz(0).start()
    cz(3).start()
    wave(8, 1)
    wave(9, 1)
    first_sweep(1)
    first_sweep(2)
    cz(1).start()
    cz(2).start()
    for xc in (1, 2):
        cz(xc).wait_recv()
        second_sweep(xc)
    pl.when(has_hi)(lambda: cx(0).wait_recv())
    pl.when(has_lo)(lambda: cx(1).wait_recv())
    for xc in (0, 3):
        cz(xc).wait_recv()
        second_sweep(xc)
    final = pltpu.make_async_copy(E2, out_e, out_sem.at[8])
    final.start()

    for level in (4, 5, 6):
        for h in range(2):
            x_sent(level, h)
        for x in range(8):
            zface(level, x).wait_send()
    for q in range(8):
        for x, first, second in planes(q):
            sums(q, x, second).wait_send()
    for r in (1, 2, 3):
        edge(r).wait_send()
    pl.when(has_lo)(lambda: cx(0).wait_send())
    pl.when(has_hi)(lambda: cx(1).wait_send())
    for xc in range(4):
        cz(xc).wait_send()
    for x in range(8):
        u_out(x).wait()
    final.wait()


def leg(forcing, start, kappa, coupling, lag):
    f32 = jnp.float32
    vmem = pltpu.VMEM
    dma = pltpu.SemaphoreType.DMA
    hbm = pl.BlockSpec(memory_space=pltpu.HBM)
    smem = pl.BlockSpec(memory_space=pltpu.SMEM)
    halo = (10, 5, 18, 8, 128)
    block = (8, 5, 16, 8, 128)
    return pl.pallas_call(
        leg_kernel,
        out_shape=(jax.ShapeDtypeStruct(block, f32), jax.ShapeDtypeStruct((4, 5, 8, 8, 128), f32)),
        in_specs=[hbm, hbm, hbm, smem, smem],
        out_specs=(hbm, hbm),
        scratch_shapes=[
            vmem(halo, f32), vmem(halo, f32), vmem(halo, f32),
            vmem(block, f32), vmem(block, f32), vmem(block, f32), vmem(block, f32),
            vmem((8, 16, 8, 128), f32), vmem((8, 16, 8, 128), f32),
            vmem((5, 2, 8, 128), f32), vmem((3, 5, 2, 8, 128), f32), vmem((5, 2, 8, 128), f32),
            vmem((4, 5, 8, 8, 128), f32), vmem((4, 8, 8, 128), f32),
            vmem((6, 5, 10, 8, 128), f32), vmem((4, 5, 8, 8, 128), f32),
            dma((8,)), dma((8,)), dma((1,)),
            dma((16,)), dma((16,)), dma((16,)), dma((16,)),
            dma((3,)), dma((3,)),
            dma((12,)), dma((12,)), dma((24,)), dma((24,)),
            dma((2,)), dma((2,)), dma((4,)), dma((4,)), dma((9,)),
        ],
        compiler_params=pltpu.CompilerParams(
            collective_id=0, has_side_effects=True, vmem_limit_bytes=56 * 2**20
        ),
        name="leg",
    )(forcing, start, kappa, coupling, lag)


def add_kernel(u_ref, e_ref, o_ref):
    for c in range(5):
        e = e_ref[0, c]
        v = u_ref[0, c].reshape(8, 2, 8, 128) + e[:, None]
        v = jnp.swapaxes(v.reshape(16, 8, 128), 0, 1)
        for n in range(2):
            for q in range(4):
                o_ref[n, c, 0, :, q * 128 : (q + 1) * 128] = v[n * 4 + q]


def add_correction(u, e):
    return pl.pallas_call(
        add_kernel,
        grid=(8,),
        out_shape=jax.ShapeDtypeStruct((2, 5, 8, 16, 512), jnp.float32),
        in_specs=[
            pl.BlockSpec((1, 5, 16, 8, 128), lambda x: (x, 0, 0, 0, 0)),
            pl.BlockSpec((1, 5, 8, 8, 128), lambda x: (x // 2, 0, 0, 0, 0)),
        ],
        out_specs=pl.BlockSpec((2, 5, 1, 16, 512), lambda x: (0, 0, x, 0, 0)),
        compiler_params=pltpu.CompilerParams(vmem_limit_bytes=32 * 2**20),
        name="add_correction",
    )(u, e)


def shards(forcing, state_start, kappa, coupling, lag):
    u, e = leg(forcing, state_start, kappa, coupling, lag)
    return add_correction(u, e)


def solution(mesh):
    return jax.shard_map(
        shards,
        mesh=mesh,
        in_specs=(
            P("instance", None, "space", "coarse", None),
            P("instance", None, "space", "coarse", None),
            P("space", "coarse", None),
            P(),
            P("coarse"),
        ),
        out_specs=P("instance", None, "space", "coarse", None),
        check_vma=False,
    )
```

time: 631 us -> 136 us (0.22)
  local copies, waits for them, and re-layouts: 206 us -> 2.82 us
  other arithmetic: 148 us -> 0 us
  Pallas kernels: 0 us -> 131 us
  starting transfers between devices: 87.6 us -> 0 us
  waiting for transfers between devices: 87 us -> 0 us
  matrix products: 80.8 us -> 0 us
  between operations: 14.5 us -> 0.02 us
    pallas_call x0 -> x2, Pallas kernels: none -> 131 us  [the longest x1 128 us: leg(): pl.pallas_call(leg_kernel, out_shape=(jax.ShapeDtypeStruct(block, f32), j...]
    ppermute x36 -> x0, starting transfers between devices: 87.6 us -> none  [the longest x18 53.7 us: with_halo(): after = lax.ppermute(leading, axis, down)]
    dot_general x12 -> x0, matrix products: 80.8 us -> none  [the longest x7 39.8 us: residual_of(): mixed = jnp.einsum('cd,ndxzy->ncxzy', coupling, field, precision=HIGH)]
    add x8 -> x0, other arithmetic: 74.5 us -> none  [the longest x5 70.6 us: shards(): begin + weight * step * residual_of(field, source, low_ghost, high_ghost,...]
    ppermute x36 -> x0, waiting for transfers between devices: 68.9 us -> none  [the longest x18 49.9 us: with_halo(): before = lax.ppermute(last, axis, up)]
    reshape x2 -> x0, local copies, waits for them, and re-layouts: 57.7 us -> none  [the longest x1 39.5 us: shards(): return field + fine_corr.reshape(inst_dev, comps, cells_x, cells_z, cells_y)]
    reduce_sum x2 -> x0, other arithmetic: 54.2 us -> none  [the longest x1 47 us: shards(): last.reshape(inst_dev, comps, half_x, 2, half_z, 2, half_y, 2)]
    slice x27 -> x0, local copies, waits for them, and re-layouts: 52.4 us -> none  [the longest x12 37.4 us: residual_of(): jnp.roll(field, -1, axis=4)]
  transfers between devices with their start and end apart: 37 -> 0, of which waited for: 24 -> 0; matrix products, arithmetic and copies ran while one was open for 57% -> 0% of each run, Pallas kernels for 0% -> 0%
where the time goes in v1:
time: 136 us; the launch traced here: 134 us
  Pallas kernels  131 us (96%)
  local copies, waits for them, and re-layouts  2.82 us (2%)
    pallas_call x1, Pallas kernels, leg(): pl.pallas_call(leg_kernel, out_shape=(jax.ShapeDtypeStruct(block, f32), j...  128 us
    pallas_call x1, Pallas kernels, add_correction(): pl.pallas_call(add_kernel, grid=(8,), out_shape=jax.ShapeDtypeStruct((2,...  3.31 us
    unnamed x4, local copies, waits for them, and re-layouts  2.82 us

profile of v1, /device:TPU:100, one launch (start us, length us, event | category | flops | bytes accessed | tf_op | source)
XLA Modules:
  0.0 133.9 jit_solution(3647088332072074182)
XLA Ops:
  0.0 127.8 %leg.1 = (f32[8,5,16,8,128]{4,3,2,1,0:T(8,128)}, f32[4,5,8,8,128]{4,3,2,1,0:T(8,128)}) custom-call(f32[2,5,8,16,512]{4,3,2,1,0:T(8,128)} %forcing.1, f32[2,5,8,16,512]{4,3,2,1,0:T(8,128)} %start.1, f32[8,16,512]{2,1,0:T(8,128)} %kappa.1, f32[5,5]{1,0:T(8,128)} %coupling.1, s32[16]{0:T(128)} %lag.1), custom_call_target="tpu_custom_call" | custom-call | tf_op jit(solution)/shard_map/leg/pallas_call | solution.py:549
  127.8 0.0 copy-start
  127.8 1.7 %copy-done = f32[8,5,16,8,128]{4,3,2,1,0:T(8,128)S(1)} copy-done((f32[8,5,16,8,128]{4,3,2,1,0:T(8,128)S(1)}, f32[8,5,16,8,128]{4,3,2,1,0:T(8,128)}, u32[]{:S(2)}) %copy-start) | copy-done | bytes 2621464
  129.5 0.0 copy-start.1
  129.5 1.1 copy-done.1
  130.6 3.3 %add_correction.1 = f32[2,5,8,16,512]{4,3,2,1,0:T(8,128)} custom-call(f32[8,5,16,8,128]{4,3,2,1,0:T(8,128)S(1)} %copy-done, f32[4,5,8,8,128]{4,3,2,1,0:T(8,128)S(1)} %copy-done.1), custom_call_target="tpu_custom_call" | custom-call | tf_op jit(solution)/shard_map/add_correction/pallas_call | solution.py:585
Async XLA Ops:
  127.8 1.7 %copy-start = (f32[8,5,16,8,128]{4,3,2,1,0:T(8,128)S(1)}, f32[8,5,16,8,128]{4,3,2,1,0:T(8,128)}, u32[]{:S(2)}) copy-start(f32[8,5,16,8,128]{4,3,2,1,0:T(8,128)} %get-tuple-element.7.u_ref) | copy-start | bytes 7864324
  129.5 1.1 copy-start.1
